TPU v7x, 512 devices: a whole 4x4x16 slice. The times are simulated.
512 devices in a mesh: row: 16 (over z), col: 32 (over x, y, core).
Axes of the slice: x: 4, y: 4, z: 16, core: 2. Of those that a mesh axis runs over, the one named last changes fastest.
Arguments:
- trail_adj: float32 [16, 768, 12288], P(None, 'col', 'row'), as said below
- trail_factor: float32 [12288, 768], P(('row', 'col')), may hold values from -0.0546875 to 0.0546875
- trail_lbar: float32 [12288, 768], P(('row', 'col')), may hold values from -6 to 6
- head_factor: float32 [6, 65536], P(None, ('row', 'col')), as said below
- head_inverse: float32 [3, 65536], P(None, ('row', 'col')), as said below
- head_lbar: float32 [6, 65536], P(None, ('row', 'col')), may hold values from -6 to 6
Outputs:
- trail_cols: float32 [12288, 768], P(('row', 'col'))
- head_adj: float32 [6, 65536], P(None, ('row', 'col'))
Inputs may be any that keep to these rules, and one draw needn't show every extreme that they name: trail_adj read as the matrix Z is exactly symmetric. The diagonal blocks F[k, k] of head_factor are lower triangular with a positive diagonal. Block k of head_inverse is lower triangular and is the inverse of F[k, k] up to float32 rounding.
All inputs are finite; a program needn't handle non-finite values.
Results may differ from a plain program's by a relative error of at most 0.00026.
Values sent between devices are 32-bit elements; how exact they have to be, the bound alone decides.
A program may use at most 64 MiB of HBM per device.

v0:
```python
import jax
import jax.numpy as jnp
from jax import lax
from jax.sharding import PartitionSpec as P

NB = 256


highest = lax.Precision.HIGHEST


def matmul(left, right):
    return jnp.dot(left, right, precision=highest, preferred_element_type=jnp.float32)


def contract_rows(left, right):
    return lax.dot_general(
        left, right, (((0,), (0,)), ((), ())), precision=highest, preferred_element_type=jnp.float32
    )


def pair_index(target, source):
    return target * (target + 1) // 2 + source


def halve_lower(matrix):
    return jnp.tril(matrix) - 0.5 * jnp.diag(jnp.diag(matrix))


def chol_adjoint(factor, inverse, totals):
    inner = halve_lower(matmul(factor.T, totals))
    mapped = matmul(matmul(inverse.T, inner), inverse)
    return 0.5 * (mapped + mapped.T)


def trail_column(column, product, lbar_rows, columns, factor_blocks, inverse_blocks, breadth):
    gradient = (
        lbar_rows[:, column * breadth : (column + 1) * breadth]
        - 2.0 * product[:, column * breadth : (column + 1) * breadth]
    )
    for source in range(column + 1, 3):
        gradient = gradient - 2.0 * matmul(
            columns[source], factor_blocks[pair_index(source, column)]
        )
    return 0.5 * matmul(gradient, inverse_blocks[column])


def trail_terms_of(column, columns, factor_rows, breadth):
    own_rows = factor_rows[:, column * breadth : (column + 1) * breadth]
    terms = [contract_rows(2.0 * columns[column], own_rows)]
    for target in range(column + 1, 3):
        terms.append(contract_rows(columns[target], own_rows))
    return terms


def head_step(column, blocks, factor_blocks, inverse_blocks, lbar_blocks, sums):
    totals = lbar_blocks[pair_index(column, column)] - sums[0]
    for target in range(column + 1, 3):
        summed = sums[target - column]
        for source in range(column + 1, 3):
            if target >= source:
                mirror = blocks[pair_index(target, source)]
            else:
                mirror = blocks[pair_index(source, target)].T
            summed = summed + matmul(mirror, factor_blocks[pair_index(source, column)])
        carried = matmul(
            lbar_blocks[pair_index(target, column)] - 2.0 * summed, inverse_blocks[column]
        )
        blocks[pair_index(target, column)] = 0.5 * carried
        totals = totals - contract_rows(carried, factor_blocks[pair_index(target, column)])
    blocks[pair_index(column, column)] = chol_adjoint(
        factor_blocks[pair_index(column, column)], inverse_blocks[column], totals
    )


def body(trail_adj, trail_factor, trail_lbar, head_factor, head_inverse, head_lbar):
    gathered = (
        lax.all_gather(head_factor, ("row", "col"), axis=1, tiled=True),
        lax.all_gather(head_inverse, ("row", "col"), axis=1, tiled=True),
        lax.all_gather(head_lbar, ("row", "col"), axis=1, tiled=True),
    )
    factor_blocks = gathered[0].reshape(6, NB, NB)
    inverse_blocks = gathered[1].reshape(3, NB, NB)
    lbar_blocks = gathered[2].reshape(6, NB, NB)
    adjoint_rows = trail_adj.reshape(-1, trail_adj.shape[2])
    factor_rows = lax.all_gather(trail_factor, "row", axis=0, tiled=True)
    product = lax.psum_scatter(
        contract_rows(adjoint_rows, factor_rows), "col", scatter_dimension=0, tiled=True
    )
    columns = [None, None, None]
    blocks = [None, None, None, None, None, None]
    for column in (2, 1, 0):
        columns[column] = trail_column(
            column, product, trail_lbar, columns, factor_blocks, inverse_blocks, NB
        )
        stacked = jnp.stack(trail_terms_of(column, columns, trail_factor, NB))
        sums = lax.psum(stacked, ("row", "col"))
        head_step(column, blocks, factor_blocks, inverse_blocks, lbar_blocks, sums)
    flattened = jnp.stack(blocks).reshape(6, NB * NB)
    share = flattened.shape[1] // (lax.axis_size("row") * lax.axis_size("col"))
    head_adj = lax.dynamic_slice_in_dim(flattened, lax.axis_index(("row", "col")) * share, share, 1)
    trail_cols = jnp.concatenate(columns, axis=1)
    return (trail_cols, head_adj)


def solution(mesh):
    in_specs = (
        P(None, "col", "row"),
        P(("row", "col"), None),
        P(("row", "col"), None),
        P(None, ("row", "col")),
        P(None, ("row", "col")),
        P(None, ("row", "col")),
    )
    out_specs = (P(("row", "col"), None), P(None, ("row", "col")))
    return jax.shard_map(body, mesh=mesh, in_specs=in_specs, out_specs=out_specs, check_vma=False)
```

profile of v0, /device:TPU:1, one launch (start us, length us, event | category | flops | bytes accessed | tf_op | source)
XLA Modules:
  0.0 1124.0 jit_solution(9694433864100573245)
XLA Ops:
  7.2 0.7 all-gather.4.cloned.1.call-update
  8.0 0.7 all-gather.6.cloned.1.call-update
  8.7 68.6 %all-gather.4.cloned.1.call-done = f32[384,768]{1,0:T(8,128)} async-done(((f32[24,768]{1,0:T(8,128)}), f32[384,768]{1,0:T(8,128)}) %all-gather.4.cloned.1.call-update) | async-done | bytes 1179664 | tf_op jit(solution)/shard_map/all_gather | solution.py:86
  77.3 6.6 fusion.59
  84.0 0.5 all-gather.8.cloned.1.call-update
  84.6 143.1 %all_gather.13 = f32[3,65536]{1,0:T(4,128)S(1)} all-gather(f32[3,128]{1,0:T(4,128)S(1)} %copy-done.7), channel_id=1, replica_groups=mesh['row'=16,'col'=32] {'row','col'}, dimensions={1}, use_global_device_ids=true | all-gather | bytes 787968 | tf_op jit(solution)/shard_map/all_gather | solution.py:79
  227.8 2.0 slice_reduce_fusion.8
  230.0 52.5 %all-gather.6.cloned.1.call-done = f32[6,65536]{1,0:T(8,128)} async-done(((f32[6,128]{1,0:T(8,128)}), f32[6,65536]{1,0:T(8,128)}) %all-gather.6.cloned.1.call-update) | async-done | bytes 1572880 | tf_op jit(solution)/shard_map/all_gather | solution.py:78
  282.5 10.3 slice_reduce_fusion
  293.0 1.0 squeeze.79
  294.0 88.9 %reduce-scatter.2.cloned.1.call-done = f32[24,768]{1,0:T(8,128)} async-done(((f32[768,768]{1,0:T(8,128)}), f32[24,768]{1,0:T(8,128)}) %reduce-scatter.2.cloned.1.call-update) | async-done | bytes 73744 | tf_op jit(solution)/shard_map/reduce_scatter | solution.py:87
  382.9 1.6 broadcast_multiply_fusion.5
  384.5 1.1 convolution_bitcast_fusion.3
  385.7 1.0 copy.26
  386.7 1.1 convolution_bitcast_fusion.6
  387.8 1.0 fusion.8
  388.8 0.8 broadcast_multiply_fusion.4
  389.7 0.4 convolution_bitcast_fusion.7
  390.1 0.4 convolution_bitcast_fusion.5
  390.5 0.4 convolution_bitcast_fusion.4
  390.9 1.0 fusion.7
  392.2 0.8 broadcast_multiply_fusion.3
  393.0 0.4 convolution_bitcast_fusion.8
  393.4 0.8 pad_maximum_fusion.1
  394.3 1.2 pad_maximum_fusion
  395.5 0.8 squeeze.90
  396.3 0.8 squeeze.91
  397.1 1.5 pad_maximum_fusion.2
  398.6 184.7 %all-gather.8.cloned.1.call-done = f32[6,65536]{1,0:T(8,128)} async-done(((f32[6,128]{1,0:T(8,128)}), f32[6,65536]{1,0:T(8,128)}) %all-gather.8.cloned.1.call-update) | async-done | bytes 1572880 | tf_op jit(solution)/shard_map/all_gather | solution.py:80
  583.3 474.4 %all-reduce.3.cloned.1.call-done = (f32[1,65536]{1,0:T(1,128)}, f32[2,256,256]{2,1,0:T(8,128)}, f32[3,256,256]{2,1,0:T(8,128)}) async-done(((f32[1,65536]{1,0:T(1,128)}, f32[2,256,256]{2,1,0:T(8,128)}, f32[3,256,256]{2,1,0:T(8,128)}), (f32[1,65536]{1,0:T(1,128)}, f32[2,256,256]{2,1,0:T(8,128)}, f32[3,256,256]{2,1,0:T(8,128)})) %all-reduce.3.cloned.1.call-update) | async-done | bytes 1572880 | tf_op jit(solution)/shard_map/psum | solution.py:97
  1057.6 11.0 slice_reduce_fusion.1
  1068.7 0.8 sub.66
  1069.5 1.5 convolution_bitcast_fusion.2
  1071.0 2.4 gather_fusion
  1073.8 0.6 fusion.60
  1074.6 1.0 squeeze.87
  1075.6 1.6 fusion.3
  1077.7 1.7 squeeze.85
  1079.4 1.6 convolution_subtract_fusion.2
  1081.1 1.5 convolution_bitcast_fusion.1
  1082.6 2.4 gather_fusion.1
  1085.0 0.4 fusion.20
  1085.4 0.6 fusion.62
  1086.3 2.3 convolution_add_fusion.3
  1088.6 2.3 convolution_add_fusion.1
  1090.8 0.7 broadcast_multiply_fusion.2
  1091.6 0.8 copy.25
  1092.5 1.6 fusion.5
  1094.4 1.0 squeeze.83
  1095.5 1.3 fusion.4
  1097.2 1.0 squeeze.81
  1098.2 0.8 copy.19
  1099.1 1.5 convolution_subtract_fusion.1
  1100.8 0.6 convolution_subtract_fusion
  1101.4 0.6 convolution_bitcast_fusion
  1102.0 2.6 gather_fusion.2
  1105.0 0.6 fusion.65
  1106.4 1.0 copy.30
  1107.5 1.0 copy.28
  1108.5 1.0 copy.29
  1109.6 1.0 copy.31
  1110.6 1.0 copy.32
  1111.6 4.8 stack.59
  1116.4 0.6 constant_dynamic-slice_fusion
  (53 shorter events, 4.7 us)
Async XLA Ops:
  7.2 70.1 %copy-start = (f32[16,24,768]{2,1,0:T(8,128)S(1)}, f32[16,24,768]{2,1,0:T(8,128)}, u32[]{:S(2)}) copy-start(f32[16,24,768]{2,1,0:T(8,128)} %param.6) | copy-start | bytes 3538948
  7.2 70.1 %all-gather.4.cloned.1.call-start = ((), (), s32[]{:S(2)}) async-start(), calls=%async_computation.1 | async-start | bytes 1253376 | tf_op jit(solution)/shard_map/all_gather | solution.py:86
  7.9 274.6 %all-gather.6.cloned.1.call-start = ((), (), s32[]{:S(2)}) async-start(), calls=%async_computation.3 | async-start | bytes 2101248 | tf_op jit(solution)/shard_map/all_gather | solution.py:78
  8.7 374.2 %reduce-scatter.2.cloned.1.call-start = ((), (), s32[]{:S(2)}) async-start(), calls=%async_computation.2 | async-start | bytes 2433024 | tf_op jit(solution)/shard_map/reduce_scatter | solution.py:87
  84.0 0.7 copy-start.7
  84.0 499.3 %all-gather.8.cloned.1.call-start = ((), (), s32[]{:S(2)}) async-start(), calls=%async_computation.4 | async-start | bytes 2101248 | tf_op jit(solution)/shard_map/all_gather | solution.py:80
  84.6 973.1 %all-reduce.3.cloned.1.call-start = ((), (), s32[]{:S(2)}) async-start(), calls=%async_computation.5 | async-start | bytes 3145728 | tf_op jit(solution)/shard_map/psum | solution.py:97
  382.9 6.8 copy-start.6
  397.1 672.3 %copy-start.1 = (f32[256,256]{1,0:T(8,128)S(1)}, f32[256,256]{1,0:T(8,128)}, u32[]{:S(2)}) copy-start(f32[256,256]{1,0:T(8,128)} %squeeze.90) | copy-start | bytes 786436
  1086.2 6.2 copy-start.5
  1105.6 1.8 copy-start.4
  1106.0 3.5 copy-start.3
  1106.3 4.3 copy-start.2
Sparse Core Ops, SparseCore 0:
  10.1 67.1 all-gather.3
  81.9 200.5 all-gather.5
  286.9 95.8 reduce-scatter.1
  388.2 195.0 all-gather.7
  589.7 467.9 all-reduce.2
where the time goes:
time: 1130 us; the launch traced here: 1120 us
  waiting for transfers between devices  871 us (77%)
  blocking collectives  143 us (13%)
  local copies, waits for them, and re-layouts  43 us (4%)
  matrix products  36.6 us (3%)
  other arithmetic  15.4 us (1%)
  between operations  14.7 us (1%)
    psum x1, waiting for transfers between devices, body(): sums = lax.psum(stacked, ('row', 'col'))  474 us
    all_gather x1, waiting for transfers between devices, body(): lax.all_gather(head_lbar, ('row', 'col'), axis=1, tiled=True)  185 us
    all_gather x1, blocking collectives, body(): lax.all_gather(head_inverse, ('row', 'col'), axis=1, tiled=True)  143 us
    reduce_scatter x1, waiting for transfers between devices, body(): lax.psum_scatter(contract_rows(adjoint_rows, factor_rows), 'col', scatter...  88.9 us
    all_gather x1, waiting for transfers between devices, body(): factor_rows = lax.all_gather(trail_factor, 'row', axis=0, tiled=True)  68.6 us
    all_gather x1, waiting for transfers between devices, body(): lax.all_gather(head_factor, ('row', 'col'), axis=1, tiled=True)  52.5 us
  transfers between devices with their start and end apart: 5, of which 5 were waited for; matrix products, arithmetic and copies ran while one was open for 3% of the time, Pallas kernels for 0%

commit v1 on v0

v1 whole, which is shorter than its diff:
```python
import functools

import jax
import jax.numpy as jnp
from jax import lax
from jax.experimental import pallas as pl
from jax.experimental.pallas import tpu as pltpu
from jax.sharding import PartitionSpec as P

MESH = pl.DeviceIdType.MESH
NB = 256
HALF = 128
NZ = 16
NQ = 16
RING = 8
STOP = 99


def dot(left, right):
    return jnp.dot(left, right, precision=lax.Precision.HIGH, preferred_element_type=jnp.float32)


def kernel(
    z_ref, f_ref, b_ref, hf_ref, hi_ref, hl_ref, xt_ref, head_ref,
    zt, fz, y, yr, pr, zslot_f, zslot_i, hx, hm, nat, nrecv, tsum, trecv, zsend, zrecv,
    ring_send, ring_recv, hz_send, hz_recv, hx_send, hx_recv, hs_sem, ys_sem, yx_send, yx_recv,
    xs_sem, xx_send, xx_recv, xz_send, xz_recv,
):
    row = lax.axis_index("row")
    col = lax.axis_index("col")
    core = lax.rem(col, 2)
    chip = col // 2
    other = 1 - core
    sibling = (row, chip * 2 + other)

    def along_row(step):
        return (lax.rem(row + step, NZ), col)

    def along_col(step):
        return (row, lax.rem(chip + step, NQ) * 2 + core)

    def remote(src, dst, send, recv, target):
        return pltpu.make_async_remote_copy(
            src_ref=src, dst_ref=dst, send_sem=send, recv_sem=recv, device_id=target, device_id_type=MESH
        )

    def wait(region, sem):
        pltpu.make_async_copy(region, region, sem).wait()

    barrier = pltpu.get_barrier_semaphore()
    pl.semaphore_signal(barrier, inc=1, device_id=sibling, device_id_type=MESH)

    def greet(step, carry):
        pl.semaphore_signal(barrier, inc=1, device_id=along_row(step), device_id_type=MESH)
        pl.semaphore_signal(barrier, inc=1, device_id=along_col(step), device_id_type=MESH)
        return carry

    lax.fori_loop(1, NZ, greet, 0)
    for panel in range(3):
        fz[panel, row] = f_ref[:, panel * NB : (panel + 1) * NB]
    zslot_f[row] = hf_ref[...]
    zslot_i[row] = hi_ref[...]
    pl.semaphore_wait(barrier, 31)

    right = along_row(1)
    left = along_row(NZ - 1)

    def ring_copy(panel, way, step):
        if way == 0:
            slot, target = lax.rem(row - step + NZ, NZ), right
        else:
            slot, target = lax.rem(row + step, NZ), left
        if step == RING - 1:
            block = fz.at[panel, slot, :, pl.ds(way * HALF, HALF)]
        else:
            block = fz.at[panel, slot]
        return remote(block, block, ring_send, ring_recv.at[way, panel, step], target)

    def ring_landed(panel, way, step):
        if step == RING - 1:
            region = fz.at[panel, 0, :, pl.ds(way * HALF, HALF)]
        else:
            region = fz.at[panel, 0]
        wait(region, ring_recv.at[way, panel, step])

    def ring_step(step):
        for panel in (2, 1, 0):
            for way in (0, 1):
                if step > 0:
                    ring_landed(panel, way, step - 1)
                ring_copy(panel, way, step).start()

    def head_send(step, carry):
        remote(hf_ref, zslot_f.at[row], hz_send, hz_recv.at[0], along_row(step)).start()
        remote(hi_ref, zslot_i.at[row], hz_send, hz_recv.at[1], along_row(step)).start()
        return carry

    def turn(slab):
        rows = z_ref[:, :, slab * HALF : (slab + 1) * HALF].reshape(NZ * 24, HALF)
        hm[slab * HALF : (slab + 1) * HALF, :] = rows.T

    ring_step(0)
    lax.fori_loop(1, NZ, head_send, 0)
    turn(0)
    turn(1)
    ring_step(1)
    turn(2)
    ring_step(2)
    turn(3)
    ring_step(3)
    turn(4)
    wait(zslot_f.at[pl.ds(0, NZ - 1)], hz_recv.at[0])
    wait(zslot_i.at[pl.ds(0, NZ - 1)], hz_recv.at[1])
    for block in range(6):
        hx[core, chip, block] = zslot_f[:, block, :]
    for block in range(3):
        hx[core, chip, 6 + block] = zslot_i[:, block, :]

    def head_spread(step, carry):
        remote(hx.at[core, chip], hx.at[core, chip], hx_send, hx_recv, along_col(step)).start()
        return carry

    lax.fori_loop(1, NQ, head_spread, 0)
    ring_step(4)
    turn(5)
    ring_step(5)
    for half in range(2):
        for part in range(NQ):
            start = (part * 2 + half) * 24
            zt[half, part * 24 : (part + 1) * 24, :] = hm[start : start + 24, :]
    ring_step(6)
    ring_step(7)
    for panel in (2, 1, 0):
        for way in (0, 1):
            ring_landed(panel, way, RING - 1)
    if STOP <= 1:
        xt_ref[...] = fz[0, 0][:, :1] + jnp.zeros_like(xt_ref)
        head_ref[...] = zt[0, :6, :128]

    head = {}
    y_copies, s_copies = {}, {}
    if STOP >= 2:
        for panel in (2, 1, 0):
            factor = fz[panel].reshape(NZ * 24, NB)
            y[panel, other] = dot(zt[other], factor).reshape(NQ, 24, NB)
            y_copies[panel] = remote(y.at[panel, other], yr.at[panel], ys_sem.at[0, panel], ys_sem.at[1, panel], sibling)
            y_copies[panel].start()
            y[panel, core] = dot(zt[core], factor).reshape(NQ, 24, NB)

    if STOP >= 3:
        for panel in (2, 1, 0):
            y_copies[panel].wait_recv()
            y[panel, core] = y[panel, core] + yr[panel]

            def spread(step, carry):
                remote(
                    y.at[panel, core, lax.rem(chip + step, NQ)], pr.at[panel, step - 1],
                    yx_send.at[panel], yx_recv.at[panel], along_col(step),
                ).start()
                return carry

            lax.fori_loop(1, NQ, spread, 0)

    wait(hx.at[0, pl.ds(0, NQ - 1)], hx_recv)
    head_copy = remote(hx.at[core], hx.at[core], hs_sem.at[0], hs_sem.at[1], sibling)
    head_copy.start()
    head_copy.wait_recv()

    blocks = []
    if STOP >= 4:
        for block in range(9):
            for half in range(2):
                rows = hx[half, :, block].reshape(NB, HALF)
                nat[half, block] = rows
            halves = []
            for half in range(2):
                pieces = [nat[half, block, pl.ds(z, NQ, stride=NQ), :] for z in range(NZ)]
                halves.append(jnp.concatenate(pieces, axis=0))
            blocks.append(jnp.concatenate(halves, axis=1))
        f_blocks, w_blocks = blocks[:6], blocks[6:]
        for block in range(6):
            head["f", block] = f_blocks[block]
        for block in range(3):
            head["w", block] = w_blocks[block]

    def pair(target, source):
        return target * (target + 1) // 2 + source

    def fb(target, source):
        return head["f", pair(target, source)]

    rows_of = lax.broadcasted_iota(jnp.int32, (NB, NB), 0)
    cols_of = lax.broadcasted_iota(jnp.int32, (NB, NB), 1)
    own_row = row * NQ + chip
    own_mask = jnp.logical_and(rows_of == own_row, cols_of // HALF == core)

    def own_share(block):
        lane = hl_ref[block : block + 1, :]
        return jnp.where(own_mask, jnp.concatenate([lane, lane], axis=1), 0.0)

    def adjoint(column, totals):
        inner = dot(fb(column, column).T, totals)
        inner = jnp.where(rows_of > cols_of, inner, jnp.where(rows_of == cols_of, 0.5 * inner, 0.0))
        mapped = dot(dot(head["w", column].T, inner), head["w", column])
        return 0.5 * (mapped + mapped.T)

    columns, terms, found, carried = {}, {}, {}, {}

    def trail(panel):
        wait(pr.at[panel], yx_recv.at[panel])
        total = y[panel, core, chip]
        for source in range(NQ - 1):
            total = total + pr[panel, source]
        gradient = b_ref[:, panel * NB : (panel + 1) * NB] - 2.0 * total
        for source in range(panel + 1, 3):
            gradient = gradient - 2.0 * dot(columns[source], fb(source, panel))
        columns[panel] = 0.5 * dot(gradient, head["w", panel])
        xt_ref[:, panel * NB : (panel + 1) * NB] = columns[panel]
        padded = jnp.concatenate([columns[panel], jnp.zeros((HALF - 24, NB), jnp.float32)], axis=0)
        turned = padded.T
        for source in range(panel + 1):
            own = f_ref[:, source * NB : (source + 1) * NB]
            own = jnp.concatenate([own, jnp.zeros((HALF - 24, NB), jnp.float32)], axis=0)
            terms[panel, source] = own_share(pair(panel, source)) - 2.0 * dot(turned, own)

    def put(panel, source, value):
        for half in range(2):
            nat[half, source] = value[:, half * HALF : (half + 1) * HALF]

    def stage(panel):
        if panel == 2:
            found[2, 2] = adjoint(2, terms[2, 2])
            carried[2, 1] = dot(terms[2, 1] - 2.0 * dot(found[2, 2], fb(2, 1)), head["w", 1])
            found[2, 1] = 0.5 * carried[2, 1]
            summed = dot(found[2, 1], fb(1, 0)) + dot(found[2, 2], fb(2, 0))
            carried[2, 0] = dot(terms[2, 0] - 2.0 * summed, head["w", 0])
            found[2, 0] = 0.5 * carried[2, 0]
        elif panel == 1:
            found[1, 1] = adjoint(1, terms[1, 1] - dot(carried[2, 1].T, fb(2, 1)))
            summed = dot(found[1, 1], fb(1, 0)) + dot(found[2, 1].T, fb(2, 0))
            carried[1, 0] = dot(terms[1, 0] - 2.0 * summed, head["w", 0])
            found[1, 0] = 0.5 * carried[1, 0]
        else:
            known = dot(carried[1, 0].T, fb(1, 0)) + dot(carried[2, 0].T, fb(2, 0))
            found[0, 0] = adjoint(0, terms[0, 0] - known)
        for source in range(panel + 1):
            for half in range(2):
                nat[half, pair(panel, source)] = found[panel, source][:, half * HALF : (half + 1) * HALF]
        first = pair(panel, 0)
        count = pl.ds(first, panel + 1)
        s_copies[panel] = remote(
            nat.at[other, count], nrecv.at[count], xs_sem.at[0, panel], xs_sem.at[1, panel], sibling
        )
        s_copies[panel].start()

    def scatter_col(panel):
        s_copies[panel].wait_recv()
        first = pair(panel, 0)
        for source in range(panel + 1):
            block = first + source
            for part in range(NQ):
                piece = nat[core, block, pl.ds(part, NZ, stride=NQ), :] + nrecv[block, pl.ds(part, NZ, stride=NQ), :]
                tsum[part, block] = piece
        count = pl.ds(first, panel + 1)

        def spread(step, carry):
            remote(
                tsum.at[lax.rem(chip + step, NQ), count], trecv.at[step - 1, count],
                xx_send.at[panel], xx_recv.at[panel], along_col(step),
            ).start()
            return carry

        lax.fori_loop(1, NQ, spread, 0)

    def scatter_row(panel):
        first = pair(panel, 0)
        count = pl.ds(first, panel + 1)
        wait(trecv.at[:, count], xx_recv.at[panel])
        total = tsum[chip, count]
        for source in range(NQ - 1):
            total = total + trecv[source, count]
        for source in range(panel + 1):
            zsend[:, first + source] = total[source].reshape(NZ, 1, HALF)

        def spread(step, carry):
            remote(
                zsend.at[lax.rem(row + step, NZ), count], zrecv.at[step - 1, count],
                xz_send.at[panel], xz_recv.at[panel], along_row(step),
            ).start()
            return carry

        lax.fori_loop(1, NZ, spread, 0)

    def finish(panel):
        first = pair(panel, 0)
        count = pl.ds(first, panel + 1)
        wait(zrecv.at[:, count], xz_recv.at[panel])
        for source in range(panel + 1):
            total = zsend[row, first + source]
            for step in range(NZ - 1):
                total = total + zrecv[step, first + source]
            head_ref[first + source : first + source + 1, :] = total

    if STOP >= 5:
        trail(2)
        stage(2)
        trail(1)
        stage(1)
        trail(0)
        stage(0)
    if STOP >= 6:
        scatter_col(2)
        scatter_col(1)
        scatter_col(0)
    if STOP >= 7:
        scatter_row(2)
        scatter_row(1)
        scatter_row(0)
        finish(2)
        finish(1)
        finish(0)

    wait(fz.at[:, pl.ds(0, NZ - 1)], ring_send)
    wait(zslot_f.at[pl.ds(0, NZ - 1)], hz_send)
    wait(zslot_i.at[pl.ds(0, NZ - 1)], hz_send)
    wait(hx.at[0, pl.ds(0, NQ - 1)], hx_send)
    head_copy.wait_send()
    for panel in range(3):
        first = pair(panel, 0)
        count = pl.ds(first, panel + 1)
        if STOP >= 2:
            y_copies[panel].wait_send()
            if STOP < 3:
                y_copies[panel].wait_recv()
        if STOP >= 3:
            wait(pr.at[panel], yx_send.at[panel])
            if STOP < 5:
                wait(pr.at[panel], yx_recv.at[panel])
        if STOP >= 5:
            s_copies[panel].wait_send()
            if STOP < 6:
                s_copies[panel].wait_recv()
        if STOP >= 6:
            wait(trecv.at[:, count], xx_send.at[panel])
            if STOP < 7:
                wait(trecv.at[:, count], xx_recv.at[panel])
        if STOP >= 7:
            wait(zrecv.at[:, count], xz_send.at[panel])
    if 1 < STOP < 5:
        xt_ref[...] = y[0, 0, 0, :, :1] + jnp.zeros_like(xt_ref)
    if 1 < STOP < 7:
        head_ref[...] = nat[0, 0, :6, :]


def scratch():
    f32 = jnp.float32
    dma = pltpu.SemaphoreType.DMA
    return [
        pltpu.VMEM((2, NQ * 24, NZ * 24), f32),
        pltpu.VMEM((3, NZ, 24, NB), f32),
        pltpu.VMEM((3, 2, NQ, 24, NB), f32),
        pltpu.VMEM((3, NQ, 24, NB), f32),
        pltpu.VMEM((3, NQ - 1, 24, NB), f32),
        pltpu.VMEM((NZ, 6, HALF), f32),
        pltpu.VMEM((NZ, 3, HALF), f32),
        pltpu.VMEM((2, NQ, 9, NZ, HALF), f32),
        pltpu.VMEM((768, NZ * 24), f32),
        pltpu.VMEM((2, 9, NB, HALF), f32),
        pltpu.VMEM((6, NB, HALF), f32),
        pltpu.VMEM((NQ, 6, NZ, HALF), f32),
        pltpu.VMEM((NQ - 1, 6, NZ, HALF), f32),
        pltpu.VMEM((NZ, 6, 1, HALF), f32),
        pltpu.VMEM((NZ - 1, 6, 1, HALF), f32),
        dma,
        dma((2, 3, RING)),
        dma,
        dma((2,)),
        dma,
        dma,
        dma((2,)),
        dma((2, 3)),
        dma((3,)),
        dma((3,)),
        dma((2, 3)),
        dma((3,)),
        dma((3,)),
        dma((3,)),
        dma((3,)),
    ]


def body(trail_adj, trail_factor, trail_lbar, head_factor, head_inverse, head_lbar):
    return tuple(
        pl.pallas_call(
            kernel,
            out_shape=(
                jax.ShapeDtypeStruct(trail_lbar.shape, jnp.float32),
                jax.ShapeDtypeStruct(head_lbar.shape, jnp.float32),
            ),
            in_specs=[pl.BlockSpec(memory_space=pltpu.VMEM)] * 6,
            out_specs=(pl.BlockSpec(memory_space=pltpu.VMEM), pl.BlockSpec(memory_space=pltpu.VMEM)),
            scratch_shapes=scratch(),
            compiler_params=pltpu.CompilerParams(
                collective_id=0, has_side_effects=True, vmem_limit_bytes=48 * 1024 * 1024
            ),
            name="chol_adjoint",
        )(trail_adj, trail_factor, trail_lbar, head_factor, head_inverse, head_lbar)
    )


def solution(mesh):
    in_specs = (
        P(None, "col", "row"),
        P(("row", "col"), None),
        P(("row", "col"), None),
        P(None, ("row", "col")),
        P(None, ("row", "col")),
        P(None, ("row", "col")),
    )
    out_specs = (P(("row", "col"), None), P(None, ("row", "col")))
    return jax.shard_map(body, mesh=mesh, in_specs=in_specs, out_specs=out_specs, check_vma=False)
```

time: 1130 us -> 90.2 us (0.08)
  waiting for transfers between devices: 871 us -> 0 us
  blocking collectives: 143 us -> 0 us
  Pallas kernels: 0 us -> 81.8 us
  local copies, waits for them, and re-layouts: 43 us -> 6.31 us
  matrix products: 36.6 us -> 0 us
  other arithmetic: 15.4 us -> 0 us
  between operations: 14.7 us -> 0.65 us
    psum x1 -> x0, waiting for transfers between devices: 474 us -> none  [body(): sums = lax.psum(stacked, ('row', 'col'))]
    all_gather x3 -> x0, waiting for transfers between devices: 306 us -> none  [the longest x1 185 us: body(): lax.all_gather(head_lbar, ('row', 'col'), axis=1, tiled=True)]
    all_gather x1 -> x0, blocking collectives: 143 us -> none  [body(): lax.all_gather(head_inverse, ('row', 'col'), axis=1, tiled=True)]
    reduce_scatter x1 -> x0, waiting for transfers between devices: 88.9 us -> none  [body(): lax.psum_scatter(contract_rows(adjoint_rows, factor_rows), 'col', scatter...]
    pallas_call x0 -> x1, Pallas kernels: none -> 81.8 us  [body(): pl.pallas_call(kernel, out_shape=(jax.ShapeDtypeStruct(trail_lbar.shape,...]
    dot_general x33 -> x0, matrix products: 36.6 us -> none  [the longest x23 22.3 us: matmul(): jnp.dot(left, right, precision=highest, preferred_element_type=jnp.float32)]
    slice x2 -> x0, local copies, waits for them, and re-layouts: 12.4 us -> none  [the longest x1 10.3 us: head_step(): factor_blocks[pair_index(column, column)]]
  transfers between devices with their start and end apart: 5 -> 0, of which waited for: 5 -> 0; matrix products, arithmetic and copies ran while one was open for 3% -> 0% of each run, Pallas kernels for 0% -> 0%
where the time goes in v1:
time: 90.2 us; the launch traced here: 88.7 us
  Pallas kernels  81.8 us (91%)
  local copies, waits for them, and re-layouts  6.31 us (7%)
    pallas_call x1, Pallas kernels, body(): pl.pallas_call(kernel, out_shape=(jax.ShapeDtypeStruct(trail_lbar.shape,...  81.8 us
    unnamed x14, local copies, waits for them, and re-layouts  6.31 us

profile of v1, /device:TPU:1, one launch (start us, length us, event | category | flops | bytes accessed | tf_op | source)
XLA Modules:
  0.0 88.7 jit_solution(15780827010248417811)
XLA Ops:
  0.6 0.0 copy-start
  0.6 1.3 %copy-done = f32[16,24,768]{2,1,0:T(8,128)S(1)} copy-done((f32[16,24,768]{2,1,0:T(8,128)S(1)}, f32[16,24,768]{2,1,0:T(8,128)}, u32[]{:S(2)}) %copy-start) | copy-done | bytes 1179672
  1.9 0.0 copy-start.1
  1.9 0.9 copy-done.1
  2.8 0.0 copy-start.2
  2.8 0.9 copy-done.2
  3.7 0.0 copy-start.3
  3.7 0.7 copy-done.3
  4.4 0.0 copy-start.4
  4.4 0.7 copy-done.4
  5.0 0.0 copy-start.5
  5.0 0.7 copy-done.5
  5.7 81.8 %chol_adjoint.1 = (f32[24,768]{1,0:T(8,128)S(1)}, f32[6,128]{1,0:T(8,128)S(1)}) custom-call(f32[16,24,768]{2,1,0:T(8,128)S(1)} %copy-done, f32[24,768]{1,0:T(8,128)S(1)} %copy-done.1, f32[24,768]{1,0:T(8,128)S(1)} %copy-done.2, f32[6,128]{1,0:T(8,128)S(1)} %copy-done.3, f32[3,128]{1,0:T(4,128)S(1)} %copy-done.5, f32[6,128]{1,0:T(8,128)S(1)} %copy-done.4), custom_call_target="tpu_custom_call" | custom-call | tf_op jit(solution)/shard_map/chol_adjoint/pallas_call | solution.py:394
  87.5 0.6 copy.10
  88.1 0.6 copy.11
Async XLA Ops:
  0.6 1.3 %copy-start = (f32[16,24,768]{2,1,0:T(8,128)S(1)}, f32[16,24,768]{2,1,0:T(8,128)}, u32[]{:S(2)}) copy-start(f32[16,24,768]{2,1,0:T(8,128)} %z_ref.1) | copy-start | bytes 3538948
  1.9 0.9 copy-start.1
  2.8 0.9 copy-start.2
  3.7 0.7 copy-start.3
  4.4 0.7 copy-start.4
  5.0 0.7 copy-start.5

commit v2 on v0

v2 whole, which is shorter than its diff:
```python
import functools

import jax
import jax.numpy as jnp
from jax import lax
from jax.experimental import pallas as pl
from jax.experimental.pallas import tpu as pltpu
from jax.sharding import PartitionSpec as P

MESH = pl.DeviceIdType.MESH
NB = 256
HALF = 128
NZ = 16
NQ = 16
REACH = 8
PLANE = (
    (1, 0), (0, 1), (3, 0), (0, 3), (1, 1), (3, 3), (1, 3), (3, 1),
    (2, 0), (0, 2), (2, 1), (1, 2), (2, 3), (3, 2), (2, 2),
)


def dot(left, right):
    return jnp.dot(left, right, precision=lax.Precision.HIGH, preferred_element_type=jnp.float32)


def kernel(
    z_hbm, f_hbm, b_hbm, hf_hbm, hi_hbm, hl_hbm, xt_ref, head_ref,
    z_ref, b_ref, hf_ref, hi_ref, hl_ref, hf_side, pack,
    zt, fz, fcol, q, qr, y, yr, pr, zslot, hx, hm, nat, nrecv, tsum, trecv, zsend, zrecv,
    in_sem, side_sem, ring_send, ring_recv, fc_send, fc_recv, fs_sem, q_send, q_recv, hz_send, hz_recv, hx_send, hx_recv, hs_sem, ys_sem, yx_send, yx_recv,
    xs_sem, xx_send, xx_recv, xz_send, xz_recv,
):
    row = lax.axis_index("row")
    col = lax.axis_index("col")
    core = lax.rem(col, 2)
    chip = col // 2
    other = 1 - core
    sibling = (row, chip * 2 + other)

    def along_row(step):
        return (lax.rem(row + step, NZ), col)

    chip_x, chip_y = chip // 4, lax.rem(chip, 4)

    def plane(index):
        first, second = PLANE[index]
        move_x = first * (1 - core) + second * core
        move_y = second * (1 - core) + first * core
        return lax.rem(chip_x + move_x, 4) * 4 + lax.rem(chip_y + move_y, 4)

    def along_col(index):
        return (row, plane(index) * 2 + core)

    def remote(src, dst, send, recv, target):
        return pltpu.make_async_remote_copy(
            src_ref=src, dst_ref=dst, send_sem=send, recv_sem=recv, device_id=target, device_id_type=MESH
        )

    def wait(region, sem):
        pltpu.make_async_copy(region, region, sem).wait()

    pending = {}

    def landed(key):
        pending.pop(key)()

    def later(key, region, sem):
        pending[key] = functools.partial(wait, region, sem)

    inputs = [
        pltpu.make_async_copy(hf_hbm, hf_ref, in_sem.at[0]),
        pltpu.make_async_copy(hi_hbm, hi_ref, in_sem.at[1]),
        pltpu.make_async_copy(f_hbm.at[:, pl.ds(0, NB)], fz.at[0, row], in_sem.at[2]),
        pltpu.make_async_copy(f_hbm.at[:, pl.ds(NB, NB)], fz.at[1, row], in_sem.at[3]),
        pltpu.make_async_copy(f_hbm.at[:, pl.ds(2 * NB, NB)], fz.at[2, row], in_sem.at[4]),
        pltpu.make_async_copy(z_hbm, z_ref, in_sem.at[5]),
        pltpu.make_async_copy(b_hbm, b_ref, in_sem.at[6]),
        pltpu.make_async_copy(hl_hbm, hl_ref, in_sem.at[7]),
    ]
    for copy in inputs:
        copy.start()

    barrier = pltpu.get_barrier_semaphore()
    pl.semaphore_signal(barrier, inc=1, device_id=sibling, device_id_type=MESH)
    for index in range(NQ - 1):
        pl.semaphore_signal(barrier, inc=1, device_id=along_col(index), device_id_type=MESH)

    def greet(step, carry):
        pl.semaphore_signal(barrier, inc=1, device_id=along_row(step), device_id_type=MESH)
        return carry

    lax.fori_loop(1, NZ, greet, 0)
    for copy in inputs[:5]:
        copy.wait()
    pack[0:1] = hf_ref[1:2]
    pack[1:3] = hf_ref[3:5]
    pack[3:6] = hi_ref[...]
    zslot[row] = pack[...]
    pl.semaphore_wait(barrier, 31)

    def ring_block(panel, way, distance, slot):
        if distance == REACH:
            return fz.at[panel, slot, :, pl.ds(way * HALF, HALF)]
        return fz.at[panel, slot]

    def ring_landed(panel, way, distance):
        landed(("ring", way, panel, distance))

    def ring_step(step):
        for panel in (1, 0):
            for way in (0, 1):
                if step > 0:
                    ring_landed(panel, way, 2 * step)
                for ahead in (2, 1):
                    distance = 2 * step + ahead
                    if way == 0:
                        slot, target = lax.rem(row - 2 * step + NZ, NZ), along_row(ahead)
                    else:
                        slot, target = lax.rem(row + 2 * step, NZ), along_row(NZ - ahead)
                    block = ring_block(panel, way, distance, slot)
                    remote(block, block, ring_send, ring_recv.at[way, panel, distance - 1], target).start()
                    later(
                        ("ring", way, panel, distance), ring_block(panel, way, distance, 0),
                        ring_recv.at[way, panel, distance - 1],
                    )

    def head_send(step, carry):
        remote(pack, zslot.at[row], hz_send, hz_recv, along_row(step)).start()
        return carry

    def turn(slab):
        rows = z_ref[:, :, slab * HALF : (slab + 1) * HALF].reshape(NZ * 24, HALF)
        hm[slab * HALF : (slab + 1) * HALF, :] = rows.T

    head = {}
    y_copies, s_copies, h_copies = {}, {}, {}

    def head_row():
        lax.fori_loop(1, NZ, head_send, 0)
        copy = remote(hf_ref, hf_side, side_sem.at[0], side_sem.at[1], sibling)
        copy.start()
        pending["side"], pending["side_out"] = copy.wait_recv, copy.wait_send
        later("hz", zslot.at[pl.ds(0, NZ - 1)], hz_recv)
        later("hz_out", zslot.at[pl.ds(0, NZ - 1)], hz_send)

    def turn_all():
        for copy in inputs[5:]:
            copy.wait()
        for slab in range(6):
            turn(slab)

    def head_col():
        landed("hz")
        for block in range(6):
            hx[core, chip, block] = zslot[:, block, :]
        for index in range(NQ - 1):
            remote(hx.at[core, chip], hx.at[core, chip], hx_send, hx_recv, along_col(index)).start()
        later("hx", hx.at[0, pl.ds(0, NQ - 1)], hx_recv)
        later("hx_out", hx.at[0, pl.ds(0, NQ - 1)], hx_send)

    def column_gather():
        fcol[core, chip] = fz[2, row]
        own = fcol.at[core, chip]
        for index in range(NQ - 1):
            remote(fz.at[2, row], own, fc_send, fc_recv, along_col(index)).start()
        later("fc", fcol.at[0, pl.ds(0, NQ - 1)], fc_recv)
        later("fc_out", fcol.at[0, pl.ds(0, NQ - 1)], fc_send)

    def column_sibling():
        landed("fc")
        copy = remote(fcol.at[core], fcol.at[core], fs_sem.at[0], fs_sem.at[1], sibling)
        copy.start()
        pending["fs"], pending["fs_out"] = copy.wait_recv, copy.wait_send

    def reduce_send(way, distance):
        slot = lax.rem(row + (NZ - distance if way else distance), NZ)
        ahead = 1 if distance % 2 else 2
        target = along_row(NZ - ahead if way else ahead)
        if distance == REACH:
            source = q.at[slot, :, pl.ds(way * HALF, HALF)]
            there = qr.at[way, distance - 1, :, pl.ds(way * HALF, HALF)]
        else:
            source, there = q.at[slot], qr.at[way, distance - 1]
        remote(source, there, q_send, q_recv.at[way, distance - 1], target).start()
        later(("q", way, distance), there, q_recv.at[way, distance - 1])

    def multiply_rows():
        landed("fs")
        factor = jnp.concatenate([fcol[side, part] for part in range(NQ) for side in range(2)], axis=0)
        q[...] = dot(z_ref[...].reshape(NZ * 24, NZ * 48), factor).reshape(NZ, 24, NB)
        for distance in (8, 7, 5, 3, 1):
            for way in range(2):
                reduce_send(way, distance)
        later("q_out", q.at[pl.ds(0, NZ - 1)], q_send)

    def reduce_step(distance):
        for way in range(2):
            slot = lax.rem(row + (NZ - distance if way else distance), NZ)
            landed(("q", way, distance + 1))
            landed(("q", way, distance + 2))
            if distance + 2 == REACH:
                lanes_of = slice(way * HALF, (way + 1) * HALF)
                q[slot] = q[slot] + qr[way, distance]
                q[slot, :, lanes_of] = q[slot, :, lanes_of] + qr[way, distance + 1, :, lanes_of]
            else:
                q[slot] = q[slot] + qr[way, distance] + qr[way, distance + 1]
            reduce_send(way, distance)

    def arrange():
        for half in range(2):
            for part in range(NQ):
                start = (part * 2 + half) * 24
                zt[half, part * 24 : (part + 1) * 24, :] = hm[start : start + 24, :]

    def multiply(panel):
        for key in [key for key in pending if key[0] == "ring" and key[2] == panel]:
            landed(key)
        factor = fz[panel].reshape(NZ * 24, NB)
        for side in (other, core):
            product = dot(zt[side], factor)
            y[panel, side] = product.reshape(NQ, 24, NB)
            if side is other:
                copy = remote(y.at[panel, side], yr.at[panel], ys_sem.at[0, panel], ys_sem.at[1, panel], sibling)
                copy.start()
                pending["ys", panel], pending["ys_out", panel] = copy.wait_recv, copy.wait_send

    def scatter_product(panel):
        landed(("ys", panel))
        y[panel, core] = y[panel, core] + yr[panel]
        for index in range(NQ - 1):
            remote(
                y.at[panel, core, plane(index)], pr.at[panel, index], yx_send.at[panel], yx_recv.at[panel],
                along_col(index),
            ).start()
        later(("yx", panel), pr.at[panel], yx_recv.at[panel])
        later(("yx_out", panel), pr.at[panel], yx_send.at[panel])

    def product_total(panel):
        if panel == 2:
            total = q[row]
            for way in range(2):
                landed(("q", way, 1))
                landed(("q", way, 2))
                total = total + qr[way, 0] + qr[way, 1]
            return total
        landed(("yx", panel))
        total = y[panel, core, chip]
        for source in range(NQ - 1):
            total = total + pr[panel, source]
        return total

    def head_sibling():
        landed("hx")
        copy = remote(hx.at[core], hx.at[core], hs_sem.at[0], hs_sem.at[1], sibling)
        copy.start()
        pending["hs"], pending["hs_out"] = copy.wait_recv, copy.wait_send

    def head_arrange():
        landed("hs")
        for block in range(6):
            halves = []
            for half in range(2):
                nat[half, block] = hx[half, :, block].reshape(NB, HALF)
                pieces = [nat[half, block, pl.ds(z, NQ, stride=NQ), :] for z in range(NZ)]
                halves.append(jnp.concatenate(pieces, axis=0))
            head[("f10", "f20", "f21", "w0", "w1", "w2")[block]] = jnp.concatenate(halves, axis=1)

    def pair(target, source):
        return target * (target + 1) // 2 + source

    columns, gradients, terms, bracket, found = {}, {}, {}, {}, {}
    rows_of = lax.broadcasted_iota(jnp.int32, (NB, NB), 0)
    cols_of = lax.broadcasted_iota(jnp.int32, (NB, NB), 1)
    top = lax.broadcasted_iota(jnp.int32, (8, NB), 0) == 0
    lanes = lax.broadcasted_iota(jnp.int32, (8, NB), 1)
    own_lanes = jnp.logical_and(top, lanes // HALF == core)
    other_lanes = jnp.logical_and(top, lanes // HALF == other)

    def wide(ref, block):
        half = ref[block : block + 1, :]
        return jnp.broadcast_to(jnp.concatenate([half, half], axis=1), (8, NB))

    def tall(rows, extra):
        return jnp.concatenate([rows, extra, jnp.zeros((HALF - 32, NB), jnp.float32)], axis=0)

    def lbar_row(block):
        return jnp.where(own_lanes, wide(hl_ref, block), 0.0)

    def factor_row(block):
        return jnp.where(own_lanes, wide(hf_ref, block), jnp.where(other_lanes, wide(hf_side, block), 0.0))

    def start_gradient(panel):
        gradient = b_ref[:, panel * NB : (panel + 1) * NB]
        for source in range(panel + 1, 3):
            gradient = gradient - 2.0 * dot(columns[source], head["f" + str(source) + str(panel)])
        gradients[panel] = gradient

    def trail(panel):
        if panel == 2:
            landed("side")
        gradient = gradients[panel] - 2.0 * product_total(panel)
        diagonal = pair(panel, panel)
        left = tall(gradient, factor_row(diagonal)).T
        terms[panel, panel] = dot(left, tall(-fz[panel, row], lbar_row(diagonal)))
        columns[panel] = 0.5 * dot(gradient, head["w" + str(panel)])
        xt_ref[:, panel * NB : (panel + 1) * NB] = columns[panel]
        if panel > 0:
            unit = jnp.where(jnp.logical_and(top, lanes == row * NQ + chip), 1.0, 0.0)
            left = tall(columns[panel], unit).T
            for source in range(panel):
                terms[panel, source] = dot(left, tall(-2.0 * fz[source, row], lbar_row(pair(panel, source))))

    def diagonal_block(column, inner):
        lower = jnp.where(rows_of > cols_of, inner, jnp.where(rows_of == cols_of, 0.5 * inner, 0.0))
        inverse = head["w" + str(column)]
        return dot(inverse.T, dot(0.5 * (lower + lower.T), inverse))

    def stage(panel):
        if panel == 2:
            found[2, 2] = diagonal_block(2, terms[2, 2])
            bracket[2, 1] = terms[2, 1] - 2.0 * dot(found[2, 2], head["f21"])
            found[2, 1] = 0.5 * dot(bracket[2, 1], head["w1"])
            bracket[2, 0] = terms[2, 0] - 2.0 * (dot(found[2, 1], head["f10"]) + dot(found[2, 2], head["f20"]))
            found[2, 0] = 0.5 * dot(bracket[2, 0], head["w0"])
        elif panel == 1:
            found[1, 1] = diagonal_block(1, terms[1, 1] - dot(bracket[2, 1].T, head["f21"]))
            bracket[1, 0] = terms[1, 0] - 2.0 * (dot(found[1, 1], head["f10"]) + dot(found[2, 1].T, head["f20"]))
            found[1, 0] = 0.5 * dot(bracket[1, 0], head["w0"])
            terms["known"] = dot(bracket[1, 0].T, head["f10"]) + dot(bracket[2, 0].T, head["f20"])
        else:
            found[0, 0] = diagonal_block(0, terms[0, 0] - terms["known"])
        for source in range(panel + 1):
            for half in range(2):
                nat[half, pair(panel, source)] = found[panel, source][:, half * HALF : (half + 1) * HALF]
        count = pl.ds(pair(panel, 0), panel + 1)
        copy = remote(nat.at[other, count], nrecv.at[count], xs_sem.at[0, panel], xs_sem.at[1, panel], sibling)
        copy.start()
        pending["xs", panel], pending["xs_out", panel] = copy.wait_recv, copy.wait_send

    def scatter_result(panel):
        landed(("xs", panel))
        first = pair(panel, 0)
        for source in range(panel + 1):
            block = first + source
            for part in range(NQ):
                rows = pl.ds(part, NZ, stride=NQ)
                tsum[part, block] = nat[core, block, rows, :] + nrecv[block, rows, :]
        count = pl.ds(first, panel + 1)
        for index in range(NQ - 1):
            remote(
                tsum.at[plane(index), count], trecv.at[index, count], xx_send.at[panel], xx_recv.at[panel],
                along_col(index),
            ).start()
        later(("xx", panel), trecv.at[:, count], xx_recv.at[panel])
        later(("xx_out", panel), trecv.at[:, count], xx_send.at[panel])

    def result_row(panel):
        landed(("xx", panel))
        first = pair(panel, 0)
        count = pl.ds(first, panel + 1)
        total = tsum[chip, count]
        for source in range(NQ - 1):
            total = total + trecv[source, count]
        for source in range(panel + 1):
            zsend[:, first + source] = total[source].reshape(NZ, 1, HALF)

        def spread(step, carry):
            remote(
                zsend.at[lax.rem(row + step, NZ), count], zrecv.at[step - 1, count],
                xz_send.at[panel], xz_recv.at[panel], along_row(step),
            ).start()
            return carry

        lax.fori_loop(1, NZ, spread, 0)
        later(("xz", panel), zrecv.at[:, count], xz_recv.at[panel])
        later(("xz_out", panel), zrecv.at[:, count], xz_send.at[panel])

    def finish(panel):
        first = pair(panel, 0)
        count = pl.ds(first, panel + 1)
        landed(("xz", panel))
        for source in range(panel + 1):
            total = zsend[row, first + source]
            for step in range(NZ - 1):
                total = total + zrecv[step, first + source]
            head_ref[first + source : first + source + 1, :] = total

    phases = [
        (column_gather,), (head_row,), (ring_step, 0), (turn_all,), (ring_step, 1), (column_sibling,), (head_col,),
        (ring_step, 2), (arrange,), (multiply_rows,), (ring_step, 3), (reduce_step, 6),
        (multiply, 1), (reduce_step, 4), (multiply, 0), (scatter_product, 1), (scatter_product, 0), (head_sibling,),
        (reduce_step, 2), (head_arrange,), (start_gradient, 2),
        (trail, 2), (stage, 2), (start_gradient, 1), (scatter_result, 2), (trail, 1), (start_gradient, 0), (stage, 1),
        (trail, 0), (stage, 0), (scatter_result, 1), (scatter_result, 0),
        (result_row, 2), (result_row, 1), (result_row, 0), (finish, 2), (finish, 1), (finish, 0),
    ]
    for phase, *argument in phases:
        phase(*argument)
    later("ring_out", fz.at[pl.ds(0, 2), pl.ds(0, NZ - 1)], ring_send)

    for key in list(pending):
        landed(key)


def scratch():
    f32 = jnp.float32
    dma = pltpu.SemaphoreType.DMA
    return [
        pltpu.VMEM((NZ, 24, 768), f32),
        pltpu.VMEM((24, 768), f32),
        pltpu.VMEM((6, HALF), f32),
        pltpu.VMEM((3, HALF), f32),
        pltpu.VMEM((6, HALF), f32),
        pltpu.VMEM((6, HALF), f32),
        pltpu.VMEM((6, HALF), f32),
        pltpu.VMEM((2, NQ * 24, NZ * 24), f32),
        pltpu.VMEM((3, NZ, 24, NB), f32),
        pltpu.VMEM((2, NQ, 24, NB), f32),
        pltpu.VMEM((NZ, 24, NB), f32),
        pltpu.VMEM((2, REACH, 24, NB), f32),
        pltpu.VMEM((2, 2, NQ, 24, NB), f32),
        pltpu.VMEM((2, NQ, 24, NB), f32),
        pltpu.VMEM((2, NQ - 1, 24, NB), f32),
        pltpu.VMEM((NZ, 6, HALF), f32),
        pltpu.VMEM((2, NQ, 6, NZ, HALF), f32),
        pltpu.VMEM((768, NZ * 24), f32),
        pltpu.VMEM((2, 6, NB, HALF), f32),
        pltpu.VMEM((6, NB, HALF), f32),
        pltpu.VMEM((NQ, 6, NZ, HALF), f32),
        pltpu.VMEM((NQ - 1, 6, NZ, HALF), f32),
        pltpu.VMEM((NZ, 6, 1, HALF), f32),
        pltpu.VMEM((NZ - 1, 6, 1, HALF), f32),
        dma((8,)),
        dma((2,)),
        dma,
        dma((2, 2, REACH)),
        dma,
        dma,
        dma((2,)),
        dma,
        dma((2, REACH)),
        dma,
        dma,
        dma,
        dma,
        dma((2,)),
        dma((2, 2)),
        dma((2,)),
        dma((2,)),
        dma((2, 3)),
        dma((3,)),
        dma((3,)),
        dma((3,)),
        dma((3,)),
    ]


def body(trail_adj, trail_factor, trail_lbar, head_factor, head_inverse, head_lbar):
    return tuple(
        pl.pallas_call(
            kernel,
            out_shape=(
                pltpu.VMEM(trail_lbar.shape, jnp.float32),
                pltpu.VMEM(head_lbar.shape, jnp.float32),
            ),
            in_specs=[pl.BlockSpec(memory_space=pltpu.HBM)] * 6,
            out_specs=(pl.BlockSpec(memory_space=pltpu.VMEM), pl.BlockSpec(memory_space=pltpu.VMEM)),
            scratch_shapes=scratch(),
            compiler_params=pltpu.CompilerParams(
                collective_id=0, has_side_effects=True, vmem_limit_bytes=60 * 1024 * 1024
            ),
            name="chol_adjoint",
        )(trail_adj, trail_factor, trail_lbar, head_factor, head_inverse, head_lbar)
    )


def solution(mesh):
    in_specs = (
        P(None, "col", "row"),
        P(("row", "col"), None),
        P(("row", "col"), None),
        P(None, ("row", "col")),
        P(None, ("row", "col")),
        P(None, ("row", "col")),
    )
    out_specs = (P(("row", "col"), None), P(None, ("row", "col")))
    return jax.shard_map(body, mesh=mesh, in_specs=in_specs, out_specs=out_specs, check_vma=False)
```

time: 1130 us -> 72.3 us (0.06)
  waiting for transfers between devices: 871 us -> 0 us
  blocking collectives: 143 us -> 0 us
  Pallas kernels: 0 us -> 70.3 us
  local copies, waits for them, and re-layouts: 43 us -> 1.23 us
  matrix products: 36.6 us -> 0 us
  other arithmetic: 15.4 us -> 0 us
  between operations: 14.7 us -> 0.64 us
    psum x1 -> x0, waiting for transfers between devices: 474 us -> none  [body(): sums = lax.psum(stacked, ('row', 'col'))]
    all_gather x3 -> x0, waiting for transfers between devices: 306 us -> none  [the longest x1 185 us: body(): lax.all_gather(head_lbar, ('row', 'col'), axis=1, tiled=True)]
    all_gather x1 -> x0, blocking collectives: 143 us -> none  [body(): lax.all_gather(head_inverse, ('row', 'col'), axis=1, tiled=True)]
    reduce_scatter x1 -> x0, waiting for transfers between devices: 88.9 us -> none  [body(): lax.psum_scatter(contract_rows(adjoint_rows, factor_rows), 'col', scatter...]
    pallas_call x0 -> x1, Pallas kernels: none -> 70.3 us  [body(): pl.pallas_call(kernel, out_shape=(pltpu.VMEM(trail_lbar.shape, jnp.float3...]
    dot_general x33 -> x0, matrix products: 36.6 us -> none  [the longest x23 22.3 us: matmul(): jnp.dot(left, right, precision=highest, preferred_element_type=jnp.float32)]
    slice x2 -> x0, local copies, waits for them, and re-layouts: 12.4 us -> none  [the longest x1 10.3 us: head_step(): factor_blocks[pair_index(column, column)]]
  transfers between devices with their start and end apart: 5 -> 0, of which waited for: 5 -> 0; matrix products, arithmetic and copies ran while one was open for 3% -> 0% of each run, Pallas kernels for 0% -> 0%
where the time goes in v2:
time: 72.3 us; the launch traced here: 72.2 us
  Pallas kernels  70.3 us (97%)
  local copies, waits for them, and re-layouts  1.23 us (2%)
    pallas_call x1, Pallas kernels, body(): pl.pallas_call(kernel, out_shape=(pltpu.VMEM(trail_lbar.shape, jnp.float3...  70.3 us

profile of v2, /device:TPU:1, one launch (start us, length us, event | category | flops | bytes accessed | tf_op | source)
XLA Modules:
  0.0 72.2 jit_solution(14210913794551122937)
XLA Ops:
  0.6 70.3 %chol_adjoint.1 = (f32[24,768]{1,0:T(8,128)S(1)}, f32[6,128]{1,0:T(8,128)S(1)}) custom-call(f32[16,24,768]{2,1,0:T(8,128)} %z_hbm.1, f32[24,768]{1,0:T(8,128)} %f_hbm.1, f32[24,768]{1,0:T(8,128)} %b_hbm.1, f32[6,128]{1,0:T(8,128)} %hf_hbm.1, f32[3,128]{1,0:T(4,128)} %hi_hbm.1, f32[6,128]{1,0:T(8,128)} %hl_hbm.1), custom_call_target="tpu_custom_call" | custom-call | tf_op jit(solution)/shard_map/chol_adjoint/pallas_call | solution.py:460
  71.0 0.6 copy.10
  71.6 0.6 copy.11

commit v3 on v2

--- a/solution.py
+++ b/solution.py
@@ -302,6 +302,10 @@
         diagonal = pair(panel, panel)
         left = tall(gradient, factor_row(diagonal)).T
         terms[panel, panel] = dot(left, tall(-fz[panel, row], lbar_row(diagonal)))
+        if panel == 1:
+            terms["inner"] = terms[1, 1] - terms["to_inner"]
+        elif panel == 0:
+            terms["last"] = terms[0, 0] - terms["to_last"]
         columns[panel] = 0.5 * dot(gradient, head["w" + str(panel)])
         xt_ref[:, panel * NB : (panel + 1) * NB] = columns[panel]
         if panel > 0:
@@ -309,6 +313,8 @@
             left = tall(columns[panel], unit).T
             for source in range(panel):
                 terms[panel, source] = dot(left, tall(-2.0 * fz[source, row], lbar_row(pair(panel, source))))
+        if panel == 1:
+            terms["cross"] = terms[1, 0] - terms["to_cross"]
 
     def diagonal_block(column, inner):
         lower = jnp.where(rows_of > cols_of, inner, jnp.where(rows_of == cols_of, 0.5 * inner, 0.0))
@@ -323,12 +329,11 @@
             bracket[2, 0] = terms[2, 0] - 2.0 * (dot(found[2, 1], head["f10"]) + dot(found[2, 2], head["f20"]))
             found[2, 0] = 0.5 * dot(bracket[2, 0], head["w0"])
         elif panel == 1:
-            found[1, 1] = diagonal_block(1, terms[1, 1] - dot(bracket[2, 1].T, head["f21"]))
-            bracket[1, 0] = terms[1, 0] - 2.0 * (dot(found[1, 1], head["f10"]) + dot(found[2, 1].T, head["f20"]))
+            found[1, 1] = diagonal_block(1, terms["inner"])
+            bracket[1, 0] = terms["cross"] - 2.0 * dot(found[1, 1], head["f10"])
             found[1, 0] = 0.5 * dot(bracket[1, 0], head["w0"])
-            terms["known"] = dot(bracket[1, 0].T, head["f10"]) + dot(bracket[2, 0].T, head["f20"])
         else:
-            found[0, 0] = diagonal_block(0, terms[0, 0] - terms["known"])
+            found[0, 0] = diagonal_block(0, terms["last"])
         for source in range(panel + 1):
             for half in range(2):
                 nat[half, pair(panel, source)] = found[panel, source][:, half * HALF : (half + 1) * HALF]
@@ -354,45 +359,52 @@
         later(("xx", panel), trecv.at[:, count], xx_recv.at[panel])
         later(("xx_out", panel), trecv.at[:, count], xx_send.at[panel])
 
-    def result_row(panel):
-        landed(("xx", panel))
-        first = pair(panel, 0)
-        count = pl.ds(first, panel + 1)
+    def result_row(group):
+        first, number = (1, 5) if group else (0, 1)
+        for panel in (2, 1) if group else (0,):
+            landed(("xx", panel))
+        count = pl.ds(first, number)
         total = tsum[chip, count]
         for source in range(NQ - 1):
             total = total + trecv[source, count]
-        for source in range(panel + 1):
+        for source in range(number):
             zsend[:, first + source] = total[source].reshape(NZ, 1, HALF)
 
         def spread(step, carry):
             remote(
                 zsend.at[lax.rem(row + step, NZ), count], zrecv.at[step - 1, count],
-                xz_send.at[panel], xz_recv.at[panel], along_row(step),
+                xz_send.at[group], xz_recv.at[group], along_row(step),
             ).start()
             return carry
 
         lax.fori_loop(1, NZ, spread, 0)
-        later(("xz", panel), zrecv.at[:, count], xz_recv.at[panel])
-        later(("xz_out", panel), zrecv.at[:, count], xz_send.at[panel])
-
-    def finish(panel):
-        first = pair(panel, 0)
-        count = pl.ds(first, panel + 1)
-        landed(("xz", panel))
-        for source in range(panel + 1):
-            total = zsend[row, first + source]
+        later(("xz", group), zrecv.at[:, count], xz_recv.at[group])
+        later(("xz_out", group), zrecv.at[:, count], xz_send.at[group])
+
+    def finish(group):
+        landed(("xz", group))
+        for block in range(1, 6) if group else (0,):
+            total = zsend[row, block]
             for step in range(NZ - 1):
-                total = total + zrecv[step, first + source]
-            head_ref[first + source : first + source + 1, :] = total
+                total = total + zrecv[step, block]
+            head_ref[block : block + 1, :] = total
+
+    def carry_over(panel):
+        if panel == 2:
+            terms["to_inner"] = dot(bracket[2, 1].T, head["f21"])
+            terms["to_cross"] = 2.0 * dot(found[2, 1].T, head["f20"])
+            terms["to_last"] = dot(bracket[2, 0].T, head["f20"])
+        else:
+            terms["to_last"] = terms["to_last"] + dot(bracket[1, 0].T, head["f10"])
 
     phases = [
         (column_gather,), (head_row,), (ring_step, 0), (turn_all,), (ring_step, 1), (column_sibling,), (head_col,),
         (ring_step, 2), (arrange,), (multiply_rows,), (ring_step, 3), (reduce_step, 6),
         (multiply, 1), (reduce_step, 4), (multiply, 0), (scatter_product, 1), (scatter_product, 0), (head_sibling,),
         (reduce_step, 2), (head_arrange,), (start_gradient, 2),
-        (trail, 2), (stage, 2), (start_gradient, 1), (scatter_result, 2), (trail, 1), (start_gradient, 0), (stage, 1),
-        (trail, 0), (stage, 0), (scatter_result, 1), (scatter_result, 0),
-        (result_row, 2), (result_row, 1), (result_row, 0), (finish, 2), (finish, 1), (finish, 0),
+        (trail, 2), (stage, 2), (start_gradient, 1), (carry_over, 2), (scatter_result, 2), (trail, 1), (start_gradient, 0), (stage, 1), (carry_over, 1),
+        (trail, 0), (scatter_result, 1), (stage, 0), (scatter_result, 0),
+        (result_row, 1), (result_row, 0), (finish, 1), (finish, 0),
     ]
     for phase, *argument in phases:
         phase(*argument)

time: 72.3 us -> 71.9 us (level)
  no operation moved by 1% of the time
where the time goes in v3:
time: 71.9 us; the launch traced here: 71.7 us
  Pallas kernels  69.9 us (97%)
  local copies, waits for them, and re-layouts  1.23 us (2%)
    pallas_call x1, Pallas kernels, body(): pl.pallas_call(kernel, out_shape=(pltpu.VMEM(trail_lbar.shape, jnp.float3...  69.9 us

profile of v3, /device:TPU:1, one launch (start us, length us, event | category | flops | bytes accessed | tf_op | source)
XLA Modules:
  0.0 71.7 jit_solution(4875550224695770386)
XLA Ops:
  0.6 69.9 %chol_adjoint.1 = (f32[24,768]{1,0:T(8,128)S(1)}, f32[6,128]{1,0:T(8,128)S(1)}) custom-call(f32[16,24,768]{2,1,0:T(8,128)} %z_hbm.1, f32[24,768]{1,0:T(8,128)} %f_hbm.1, f32[24,768]{1,0:T(8,128)} %b_hbm.1, f32[6,128]{1,0:T(8,128)} %hf_hbm.1, f32[3,128]{1,0:T(4,128)} %hi_hbm.1, f32[6,128]{1,0:T(8,128)} %hl_hbm.1), custom_call_target="tpu_custom_call" | custom-call | tf_op jit(solution)/shard_map/chol_adjoint/pallas_call | solution.py:472
  70.5 0.6 copy.10
  71.1 0.6 copy.11
